TPU v7x, 256 devices: a whole 4x4x8 slice. The times are simulated.
256 devices in a mesh: row: 16 (over x_hi, y, core), col: 16 (over x_lo, z).
Axes of the slice: x: 4 (x_hi: 2, x_lo: 2; x = x_hi * 2 + x_lo), y: 4, z: 8, core: 2. Of those that a mesh axis runs over, the one named last changes fastest.
Arguments:
- amplitudes: bfloat16 [2048, 8, 2048], P('row', None, 'col'), may hold values from -6 to 6
- factors: bfloat16 [16, 2048, 2048], P(None, 'row', 'col'), may hold values from -0.0625 to 0.0625
- virt_irrep: int32 [32], replicated, may hold values from 0 to 1
- occupied_symmetry_label: int32 [200], replicated, may hold values from 0 to 1
- pair_index: int32 [8, 2], replicated, may hold values from 0 to 199
Outputs:
- ladder: bfloat16 [2048, 8, 2048], P('row', None, 'col')
All inputs are finite; a program needn't handle non-finite values.
Results may differ from a plain program's by a relative error of at most 0.0049.
Values may be sent and summed in bfloat16 or wider, within the bound.
A program may use at most 64 MiB of HBM per device.

v0:
```python
import jax
import jax.numpy as jnp
from jax import lax
from jax.sharding import PartitionSpec as P

NV = 2048
VB = 64


def lookup(index_entries, table):
    places = jnp.arange(table.shape[0], dtype=jnp.int32)
    hits = index_entries[..., None] == places
    return jnp.sum(jnp.where(hits, table, 0), axis=-1)


def on_device(amplitudes, factors, virt_irrep, occupied_symmetry_label, pair_index):
    rows, pairs, width = amplitudes.shape
    groups = factors.shape[0]
    row_start = lax.axis_index("row") * rows
    col_start = lax.axis_index("col") * width
    row_ids = (row_start + jnp.arange(rows, dtype=jnp.int32)) // VB
    col_ids = (col_start + jnp.arange(width, dtype=jnp.int32)) // VB
    lab_rows = lookup(row_ids, virt_irrep)
    lab_cols = lookup(col_ids, virt_irrep)
    lab_pair = lookup(pair_index[:, 0], occupied_symmetry_label) + lookup(
        pair_index[:, 1], occupied_symmetry_label
    )
    pair_parity_sign = lab_rows[:, None, None] + lab_pair[None, :, None] + lab_cols[None, None, :]
    allowed = (pair_parity_sign % 2 == 0).astype(jnp.float32)
    masked_terms = (amplitudes.astype(jnp.float32) * allowed).astype(jnp.bfloat16)
    panel = lax.all_gather(masked_terms, "col", axis=2, tiled=True)
    flat_panel = panel.reshape(rows * pairs, NV)
    halves = []
    panels = []
    summed = jnp.einsum(
        "md,qdb->qmb",
        flat_panel,
        lax.all_gather(factors, "row", axis=1, tiled=True),
        preferred_element_type=jnp.float32,
    )
    halves.append(summed.astype(jnp.bfloat16).reshape(groups, rows, pairs, width))
    panels.append(lax.all_gather(factors, "col", axis=2, tiled=True))
    result = jnp.zeros((rows * lax.axis_size("row"), pairs * width), jnp.float32)
    for half_block, panel_block in zip(halves, panels):
        picked = half_block
        picked = picked.reshape(half_block.shape[0], rows, pairs * width)
        result = jnp.einsum("qca,qcn->an", panel_block, picked, preferred_element_type=jnp.float32)
    full = lax.psum_scatter(result, "row", scatter_dimension=0, tiled=True)
    full = full.reshape(rows, pairs, width)
    return (allowed * full).astype(jnp.bfloat16)


def solution(mesh):
    in_specs = (P("row", None, "col"), P(None, "row", "col"), P(), P(), P())
    out_specs = P("row", None, "col")
    return jax.shard_map(
        on_device, mesh=mesh, in_specs=in_specs, out_specs=out_specs, check_vma=False
    )
```

profile of v0, /device:TPU:1, one launch (start us, length us, event | category | flops | bytes accessed | tf_op | source)
XLA Modules:
  0.0 440.0 jit_solution(6260400313923417153)
XLA Ops:
  6.5 0.0 all-gather.4.cloned.1.call-start
  6.5 0.8 slice_bitcast_fusion.1
  7.3 0.9 select_reduce_fusion.2
  8.2 0.7 select_reduce_fusion.1
  9.0 0.1 broadcast_add_fusion
  9.0 2.0 select_convert_fusion.1
  11.0 0.0 all-gather.4.cloned.1.call-update
  11.1 0.0 all-gather.6.cloned.1.call-start
  11.1 0.7 all-gather.6.cloned.1.call-update
  11.8 0.0 all-gather.8.cloned.1.call-start
  11.9 0.7 all-gather.8.cloned.1.call-update
  12.6 0.0 reduce-scatter.2.cloned.1.call-start
  12.6 82.0 %all-gather.4.cloned.1.call-done = bf16[128,8,2048]{2,1,0:T(8,128)(2,1)} async-done(((bf16[128,8,128]{2,1,0:T(8,128)(2,1)}), bf16[128,8,2048]{2,1,0:T(8,128)(2,1)}) %all-gather.4.cloned.1.call-update) | async-done | bytes 4194320 | tf_op jit(solution)/shard_map/all_gather | solution.py:31
  94.6 90.2 %all-gather.6.cloned.1.call-done = bf16[16,2048,128]{2,1,0:T(8,128)(2,1)} async-done(((bf16[16,128,128]{2,1,0:T(8,128)(2,1)}), bf16[16,2048,128]{2,1,0:T(8,128)(2,1)}) %all-gather.6.cloned.1.call-update) | async-done | bytes 8388624 | tf_op jit(solution)/shard_map/all_gather | solution.py:38
  184.9 13.8 %convert_bitcast_fusion = bf16[16,1024,128]{2,1,0:T(8,128)(2,1)} fusion(bf16[16,2048,128]{2,1,0:T(8,128)(2,1)} %all-gather.6.cloned.1.call-done, bf16[128,8,2048]{2,1,0:T(8,128)(2,1)} %all-gather.4.cloned.1.call-done), kind=kOutput, calls=%fused_computation.3 | convolution fusion | flops 8592031744 | bytes 16777216 | tf_op jit(solution)/shard_map/md,qdb->qmb/dot_general | solution.py:35
  198.7 7.3 %reshape_reshape.3 = bf16[16,128,1024]{2,1,0:T(8,128)(2,1)} reshape(bf16[16,1024,128]{2,1,0:T(8,128)(2,1)} %convert_bitcast_fusion) | data formatting | bytes 8388608 | tf_op jit(solution)/shard_map/reshape;reshape | solution.py:46
  206.0 97.0 %all-gather.8.cloned.1.call-done = bf16[16,128,2048]{2,1,0:T(8,128)(2,1)} async-done(((bf16[16,128,128]{2,1,0:T(8,128)(2,1)}), bf16[16,128,2048]{2,1,0:T(8,128)(2,1)}) %all-gather.8.cloned.1.call-update) | async-done | bytes 8388624 | tf_op jit(solution)/shard_map/all_gather | solution.py:42
  303.0 14.6 %convolution_bitcast_fusion = f32[2048,1024]{0,1:T(8,128)} fusion(bf16[16,128,1024]{2,1,0:T(8,128)(2,1)} %reshape_reshape.3, bf16[16,128,2048]{2,1,0:T(8,128)(2,1)} %all-gather.8.cloned.1.call-done), kind=kOutput, calls=%fused_computation | convolution fusion | flops 8589934592 | bytes 20971520 | tf_op jit(solution)/shard_map/qca,qcn->an/dot_general | solution.py:47
  317.5 0.0 reduce-scatter.2.cloned.1.call-update
  317.6 113.6 %reduce-scatter.2.cloned.1.call-done = f32[128,1024]{0,1:T(8,128)} async-done(((f32[2048,1024]{0,1:T(8,128)}), f32[128,1024]{0,1:T(8,128)}) %reduce-scatter.2.cloned.1.call-update) | async-done | bytes 524304 | tf_op jit(solution)/shard_map/reduce_scatter | solution.py:48
  431.2 1.3 copy.9
  432.4 1.0 select_convert_fusion
  (2 shorter events, 0.0 us)
Async XLA Ops:
  6.5 88.1 %all-gather.4.cloned.1.call-start = ((), (), s32[]{:S(2)}) async-start(), calls=%async_computation.1 | async-start | bytes 4456448 | tf_op jit(solution)/shard_map/all_gather | solution.py:31
  11.1 173.8 %all-gather.6.cloned.1.call-start = ((), (), s32[]{:S(2)}) async-start(), calls=%async_computation.2 | async-start | bytes 8912896 | tf_op jit(solution)/shard_map/all_gather | solution.py:38
  11.8 291.2 %all-gather.8.cloned.1.call-start = ((), (), s32[]{:S(2)}) async-start(), calls=%async_computation.3 | async-start | bytes 8912896 | tf_op jit(solution)/shard_map/all_gather | solution.py:42
  12.6 418.6 %reduce-scatter.2.cloned.1.call-start = ((), (), s32[]{:S(2)}) async-start(), calls=%async_computation.4 | async-start | bytes 8912896 | tf_op jit(solution)/shard_map/reduce_scatter | solution.py:48
Sparse Core Ops, SparseCore 0:
  11.2 83.4 all-gather.3
  97.4 87.3 all-gather.5
  186.6 116.3 all-gather.7
  317.7 113.4 reduce-scatter.1
where the time goes:
time: 440 us
  waiting for transfers between devices  384 us (87%)
  matrix products  28.3 us (6%)
  between operations  13.1 us (3%)
  local copies, waits for them, and re-layouts  9.32 us (2%)
  other arithmetic  4.78 us (1%)
    reduce_scatter x1, waiting for transfers between devices, on_device(): full = lax.psum_scatter(result, 'row', scatter_dimension=0, tiled=True)  114 us
    all_gather x1, waiting for transfers between devices, on_device(): panels.append(lax.all_gather(factors, 'col', axis=2, tiled=True))  97 us
    all_gather x1, waiting for transfers between devices, on_device(): lax.all_gather(factors, 'row', axis=1, tiled=True)  90.2 us
    all_gather x1, waiting for transfers between devices, on_device(): panel = lax.all_gather(masked_terms, 'col', axis=2, tiled=True)  82 us
    dot_general x1, matrix products, on_device(): jnp.einsum('qca,qcn->an', panel_block, picked, preferred_element_type=jnp...  14.6 us
    dot_general x1, matrix products, on_device(): jnp.einsum('md,qdb->qmb', flat_panel, lax.all_gather(factors, 'row', axis...  13.8 us
  transfers between devices with their start and end apart: 4, of which 4 were waited for; matrix products, arithmetic and copies ran while one was open for 5% of the time, Pallas kernels for 0%

commit v1 on v0

v1 whole, which is shorter than its diff:
```python
import functools

import jax
import jax.numpy as jnp
from jax import lax
from jax.experimental import pallas as pl
from jax.experimental.pallas import tpu as pltpu
from jax.sharding import PartitionSpec as P

NV = 2048
VB = 64
MESH = pl.DeviceIdType.MESH
N_SEMS = 112


def lookup(index_entries, table):
    places = jnp.arange(table.shape[0], dtype=jnp.int32)
    hits = index_entries[..., None] == places
    return jnp.sum(jnp.where(hits, table, 0), axis=-1)


def kernel(
    t_ref, ft_ref, f_ref, out_ref,
    t_all, fca, fdb, ht, rp, ra1, ra2, rb1, rb2, rc1, rc2, fin, fin_in,
    send, recv,
):
    row, col = lax.axis_index("row"), lax.axis_index("col")
    xh, y, k = row // 8, (row // 2) % 4, row % 2
    xl, z = col // 8, col % 8
    x = xh * 2 + xl

    def dev(x_to, y_to, z_to, k_to):
        return {"row": (x_to // 2) * 8 + y_to * 2 + k_to, "col": (x_to % 2) * 8 + z_to}

    def wrap(v, n):
        return lax.rem(v + n, n)

    xs = {s: wrap(x + s, 4) for s in (-1, 0, 1, 2)}
    ys = {s: wrap(y + s, 4) for s in (-1, 0, 1, 2)}
    zs = {s: wrap(z + s, 8) for s in range(-4, 5)}
    near = {
        "x": {s: dev(xs[s], y, z, k) for s in (-1, 1)},
        "y": {s: dev(x, ys[s], z, k) for s in (-1, 1)},
        "z": {s: dev(x, y, zs[s], k) for s in (-1, 1)},
    }
    sibling = dev(x, y, z, 1 - k)
    partner = dev(xh * 2 + k, y, z, xl)
    swapped = xl != k

    count = [0]
    pending = []

    def put(src, dst, device):
        number = count[0]
        count[0] += 1
        copy = pltpu.make_async_remote_copy(
            src_ref=src, dst_ref=dst, send_sem=send.at[number], recv_sem=recv.at[number],
            device_id=device, device_id_type=MESH,
        )
        copy.start()
        pending.append(copy)
        return copy

    barrier = pltpu.get_barrier_semaphore()
    for target in [*near["x"].values(), *near["y"].values(), *near["z"].values(), sibling]:
        pl.semaphore_signal(barrier, inc=1, device_id=target, device_id_type=MESH)

    @pl.when(swapped)
    def _():
        pl.semaphore_signal(barrier, inc=1, device_id=partner, device_id_type=MESH)
        pl.semaphore_wait(barrier, 8)

    @pl.when(jnp.logical_not(swapped))
    def _():
        pl.semaphore_wait(barrier, 7)

    moves = []
    for src, dst in (
        (t_ref, t_all.at[col]),
        (ft_ref, fdb.at[xh, y, k]),
        (f_ref, fca.at[col]),
    ):
        number = count[0]
        count[0] += 1
        far = pltpu.make_async_remote_copy(
            src_ref=src, dst_ref=dst, send_sem=send.at[number], recv_sem=recv.at[number],
            device_id=partner, device_id_type=MESH,
        )
        near_copy = pltpu.make_async_copy(src, dst, recv.at[number])
        moves.append((far, near_copy))

        @pl.when(swapped)
        def _():
            far.start()

        @pl.when(jnp.logical_not(swapped))
        def _():
            near_copy.start()

    def own_here(i):
        far, near_copy = moves[i]

        @pl.when(swapped)
        def _():
            far.wait_recv()

        @pl.when(jnp.logical_not(swapped))
        def _():
            near_copy.wait()

    ring_wait = {}
    side_wait = {"t": [], "f": []}

    def part(name, shard, half):
        buf = t_all if name == "t" else fca
        at = k * 8 + shard
        rows = buf.shape[1]
        if half is None:
            return buf.at[at]
        return buf.at[at, pl.ds(half * (rows // 2), rows // 2)]

    def ring_send(name, step):
        for sign in (1, -1):
            shard = zs[-sign * (step - 1)]
            piece = part(name, shard, None if step < 4 else (1 - sign) // 2)
            ring_wait[name, step, sign] = put(piece, piece, near["z"][sign])

    def side_send(name, shard, half=None):
        piece = part(name, shard, half)
        side_wait[name].append(put(piece, piece, sibling))

    def ring_step(name, step):
        for sign in (1, -1):
            ring_wait[name, step, sign].wait_recv()
        if step < 4:
            ring_send(name, step + 1)
            for sign in (1, -1):
                side_send(name, zs[-sign * step])
        else:
            side_send(name, zs[4])

    def cell(half, u, v):
        a, b = (u, v) if half == 0 else (v, u)
        return a // 2, b, a % 2

    axes = {0: ("x", "y", xs, ys), 1: ("y", "x", ys, xs)}

    def shard_of(half, u, v, quarter=None):
        start = half * 8 if quarter is None else half * 8 + quarter * 4
        return fdb.at[(*cell(half, u, v), pl.ds(start, 8 if quarter is None else 4))]

    first, second, across, across2 = {}, {}, {}, {}

    def along_v(half, i):
        u_axis, v_axis, us, vs = axes[half]
        piece = shard_of(half, us[(0, -1, 1, 2)[i]], vs[0])
        for sign in (1, -1):
            across[half, i, sign] = put(piece, piece, near[v_axis][sign])

    def plane_start(half):
        u_axis, _, us, vs = axes[half]
        piece = shard_of(half, us[0], vs[0])
        for sign in (1, -1):
            first[half, sign] = put(piece, piece, near[u_axis][sign])

    def plane_first(half):
        u_axis, _, us, vs = axes[half]
        for sign in (1, -1):
            first[half, sign].wait_recv()
            piece = shard_of(half, us[-sign], vs[0], (1 - sign) // 2)
            second[half, sign] = put(piece, piece, near[u_axis][sign])
        along_v(half, 1)
        along_v(half, 2)

    def plane_second(half):
        for sign in (1, -1):
            second[half, sign].wait_recv()
        along_v(half, 3)

    def plane_across(half, i):
        _, v_axis, us, vs = axes[half]
        for sign in (1, -1):
            across[half, i, sign].wait_recv()
            piece = shard_of(half, us[(0, -1, 1, 2)[i]], vs[-sign], (1 - sign) // 2)
            across2[half, i, sign] = put(piece, piece, near[v_axis][sign])

    def both(step, *args):
        for half in (0, 1):
            step(half, *args)

    own_here(0)
    ring_send("t", 1)
    side_send("t", zs[0])
    own_here(1)
    both(plane_start)
    both(along_v, 0)
    ring_step("t", 1)
    own_here(2)
    ring_send("f", 1)
    side_send("f", zs[0])
    ring_step("t", 2)
    both(plane_first)
    ring_step("t", 3)
    both(plane_across, 0)
    ring_step("t", 4)
    both(plane_second)
    ring_step("f", 1)
    both(plane_across, 1)
    both(plane_across, 2)
    ring_step("f", 2)
    both(plane_across, 3)
    for copy in side_wait["t"]:
        copy.wait_recv()

    def stage1(half):
        for i in range(4):
            for sign in (1, -1):
                across2[half, i, sign].wait_recv()

        def body(n, _):
            lhs = jnp.concatenate(
                [
                    fdb[r // 8, (r // 2) % 4, r % 2, half * 8 : half * 8 + 8].reshape(1024, 128)
                    for r in range(16)
                ],
                axis=1,
            )
            rhs = t_all[:, :, pl.ds(pl.multiple_of(n * 256, 256), 256)].reshape(2048, 256)
            out = jnp.dot(lhs, rhs, preferred_element_type=jnp.float32).astype(jnp.bfloat16)
            for i in range(2):
                rows = pl.ds(pl.multiple_of(n * 256 + i * 128, 128), 128)
                for j in range(8):
                    at = (half * 8 + j) * 128
                    ht[rows, at : at + 128] = out[j * 128 : j * 128 + 128, i * 128 : i * 128 + 128]
            return 0

        lax.fori_loop(0, 4, body, 0)

    stage1(0)
    ring_step("f", 3)
    stage1(1)
    ring_step("f", 4)
    for copy in side_wait["f"]:
        copy.wait_recv()

    def stage2(lo, hi):
        def body(n, _):
            y_to = wrap(y + 2 + n // 2, 4)
            xh_to = lax.rem(n, 2)
            r = xh_to * 8 + y_to * 2
            rhs = jnp.concatenate(
                [fca[r].reshape(2048, 128), fca[r + 1].reshape(2048, 128)], axis=1
            )
            out = jnp.dot(ht[...], rhs, preferred_element_type=jnp.float32).astype(jnp.bfloat16)
            rp[xh_to, y_to, 0] = out[:, :128]
            rp[xh_to, y_to, 1] = out[:, 128:]
            return 0

        lax.fori_loop(lo, hi, body, 0)

    def strip(half, v, start, size):
        if half == 0:
            return (slice(None), v, slice(None), pl.ds(start, size))
        return (v // 2, slice(None), v % 2, pl.ds(start, size))

    sums1, sums2, last1, last2 = {}, {}, {}, {}
    got1, got2 = {0: ra1, 1: rb1}, {0: ra2, 1: rb2}
    scatter = {0: ("y", "x", ys, xs), 1: ("x", "y", xs, ys)}

    def slot(sign):
        return (1 - sign) // 2

    def quarter(half, sign):
        return half * 512 + slot(sign) * 256

    def one(half, u):
        return (u // 2, y, u % 2) if half == 0 else (x // 2, u, x % 2)

    def f32(v):
        return v.astype(jnp.float32)

    def sum_first(half):
        axis, _, vs, _ = scatter[half]
        for sign in (1, -1):
            src = rp.at[strip(half, vs[2], quarter(half, sign), 256)]
            sums1[half, sign] = put(src, got1[half].at[slot(sign)], near[axis][sign])

    def sum_second(half):
        axis, _, vs, _ = scatter[half]
        for sign in (1, -1):
            sums1[half, sign].wait_recv()
            at = strip(half, vs[sign], quarter(half, sign), 256)
            rp[at] = (f32(rp[at]) + f32(got1[half][slot(sign)])).astype(jnp.bfloat16)
            src = rp.at[strip(half, vs[sign], half * 512, 512)]
            sums2[half, sign] = put(src, got2[half].at[slot(sign)], near[axis][sign])

    def sum_third(half):
        _, axis, vs, us = scatter[half]
        for sign in (1, -1):
            sums2[half, sign].wait_recv()
        at = strip(half, vs[0], half * 512, 512)
        rp[at] = (f32(rp[at]) + f32(got2[half][0]) + f32(got2[half][1])).astype(jnp.bfloat16)
        for sign in (1, -1):
            src = rp.at[(*one(half, us[2]), pl.ds(quarter(half, sign), 256))]
            last1[half, sign] = put(src, rc1.at[half, slot(sign)], near[axis][sign])

    def sum_fourth(half):
        _, axis, _, us = scatter[half]
        for sign in (1, -1):
            last1[half, sign].wait_recv()
            at = (*one(half, us[sign]), pl.ds(quarter(half, sign), 256))
            rp[at] = (f32(rp[at]) + f32(rc1[half, slot(sign)])).astype(jnp.bfloat16)
            src = rp.at[(*one(half, us[sign]), pl.ds(half * 512, 512))]
            last2[half, sign] = put(src, rc2.at[half, slot(sign)], near[axis][sign])

    def sum_last(half):
        _, _, _, us = scatter[half]
        for sign in (1, -1):
            last2[half, sign].wait_recv()
        rows = pl.ds(half * 512, 512)
        mine = f32(rp[(*one(half, us[0]), rows)])
        fin[rows, :] = (mine + f32(rc2[half, 0]) + f32(rc2[half, 1])).astype(jnp.bfloat16)

    stage2(0, 2)
    sum_first(0)
    stage2(2, 8)
    sum_first(1)
    both(sum_second)
    both(sum_third)
    both(sum_fourth)
    both(sum_last)

    number = count[0]
    back = pltpu.make_async_remote_copy(
        src_ref=fin, dst_ref=fin_in, send_sem=send.at[number], recv_sem=recv.at[number],
        device_id=partner, device_id_type=MESH,
    )

    @pl.when(swapped)
    def _():
        back.start()
        back.wait()
        out_ref[...] = fin_in[...]
        for far, _ in moves:
            far.wait_send()

    @pl.when(jnp.logical_not(swapped))
    def _():
        out_ref[...] = fin[...]

    for copy in pending:
        copy.wait_send()


def ladder(t, ft, f):
    bf16 = jnp.bfloat16
    hbm, vmem = pl.BlockSpec(memory_space=pl.ANY), pl.BlockSpec(memory_space=pltpu.VMEM)
    return pl.pallas_call(
        kernel,
        out_shape=jax.ShapeDtypeStruct((1024, 128), bf16),
        in_specs=[hbm, hbm, hbm],
        out_specs=vmem,
        scratch_shapes=[
            pltpu.VMEM((16, 128, 1024), bf16),
            pltpu.VMEM((16, 16, 128, 128), bf16),
            pltpu.VMEM((2, 4, 2, 16, 128, 128), bf16),
            pltpu.VMEM((1024, 2048), bf16),
            pltpu.VMEM((2, 4, 2, 1024, 128), bf16),
            pltpu.VMEM((2, 2, 2, 256, 128), bf16),
            pltpu.VMEM((2, 2, 2, 512, 128), bf16),
            pltpu.VMEM((2, 4, 256, 128), bf16),
            pltpu.VMEM((2, 4, 512, 128), bf16),
            pltpu.VMEM((2, 2, 256, 128), bf16),
            pltpu.VMEM((2, 2, 512, 128), bf16),
            pltpu.VMEM((1024, 128), bf16),
            pltpu.VMEM((1024, 128), bf16),
            pltpu.SemaphoreType.DMA((N_SEMS,)),
            pltpu.SemaphoreType.DMA((N_SEMS,)),
        ],
        compiler_params=pltpu.CompilerParams(
            collective_id=0, has_side_effects=True, vmem_limit_bytes=56 * 1024 * 1024
        ),
    )(t, ft, f)


def on_device(amplitudes, factors, virt_irrep, occupied_symmetry_label, pair_index):
    rows, pairs, width = amplitudes.shape
    row_start = lax.axis_index("row") * rows
    col_start = lax.axis_index("col") * width
    row_ids = (row_start + jnp.arange(rows, dtype=jnp.int32)) // VB
    col_ids = (col_start + jnp.arange(width, dtype=jnp.int32)) // VB
    lab_rows = lookup(row_ids, virt_irrep)
    lab_cols = lookup(col_ids, virt_irrep)
    lab_pair = lookup(pair_index[:, 0], occupied_symmetry_label) + lookup(
        pair_index[:, 1], occupied_symmetry_label
    )
    parity = lab_rows[:, None, None] + lab_pair[None, :, None] + lab_cols[None, None, :]
    allowed = parity % 2 == 0
    zero = jnp.zeros((), jnp.bfloat16)
    masked = jnp.where(allowed, amplitudes, zero)
    t = masked.transpose(2, 1, 0).reshape(width, pairs * rows)
    full = ladder(t, factors.transpose(0, 2, 1), factors)
    full = full.reshape(pairs, width, rows).transpose(2, 0, 1)
    return jnp.where(allowed, full, zero)


def solution(mesh):
    in_specs = (P("row", None, "col"), P(None, "row", "col"), P(), P(), P())
    out_specs = P("row", None, "col")
    return jax.shard_map(
        on_device, mesh=mesh, in_specs=in_specs, out_specs=out_specs, check_vma=False
    )
```

time: 440 us -> 143 us (0.33)
  waiting for transfers between devices: 384 us -> 0 us
  Pallas kernels: 0 us -> 134 us
  matrix products: 28.3 us -> 0 us
  between operations: 13.1 us -> 0.06 us
    all_gather x3 -> x0, waiting for transfers between devices: 269 us -> none  [the longest x1 97 us: on_device(): panels.append(lax.all_gather(factors, 'col', axis=2, tiled=True))]
    pallas_call x0 -> x1, Pallas kernels: none -> 134 us  [ladder(): pl.pallas_call(kernel, out_shape=jax.ShapeDtypeStruct((1024, 128), bf16),...]
    reduce_scatter x1 -> x0, waiting for transfers between devices: 114 us -> none  [on_device(): full = lax.psum_scatter(result, 'row', scatter_dimension=0, tiled=True)]
    dot_general x2 -> x0, matrix products: 28.3 us -> none  [the longest x1 14.6 us: on_device(): jnp.einsum('qca,qcn->an', panel_block, picked, preferred_element_type=jnp...]
    another operation x1 -> x0, local copies, waits for them, and re-layouts: 7.29 us -> none  [on_device(): picked = picked.reshape(half_block.shape[0], rows, pairs * width)]
  transfers between devices with their start and end apart: 4 -> 0, of which waited for: 4 -> 0; matrix products, arithmetic and copies ran while one was open for 5% -> 0% of each run, Pallas kernels for 0% -> 0%
where the time goes in v1:
time: 143 us; the launch traced here: 142 us
  Pallas kernels  134 us (94%)
  local copies, waits for them, and re-layouts  5.18 us (4%)
  other arithmetic  2.73 us (2%)
    pallas_call x1, Pallas kernels, ladder(): pl.pallas_call(kernel, out_shape=jax.ShapeDtypeStruct((1024, 128), bf16),...  134 us
    unnamed x10, local copies, waits for them, and re-layouts  3.8 us

profile of v1, /device:TPU:1, one launch (start us, length us, event | category | flops | bytes accessed | tf_op | source)
XLA Modules:
  0.0 142.4 jit_solution(10126765789123746462)
XLA Ops:
  0.0 0.0 copy-start.3
  0.0 0.6 copy-done.3
  0.7 0.1 select_reduce_fusion.1
  0.8 0.0 copy-start.2
  0.8 0.7 copy-done.2
  1.4 0.0 copy-start.1
  1.4 0.7 copy-done.1
  2.1 0.2 select_reduce_fusion.2
  2.3 0.1 broadcast_add_fusion
  2.4 1.3 select_bitcast_fusion
  3.7 0.0 copy-start
  3.7 0.2 copy.9
  4.0 0.8 copy.14
  4.7 0.0 copy-done
  4.8 1.0 copy.10
  5.8 134.4 %shard_map.55 = bf16[1024,128]{1,0:T(8,128)(2,1)} custom-call(bf16[128,1024]{1,0:T(8,128)(2,1)} %bitcast.16, bf16[16,128,128]{2,1,0:T(8,128)(2,1)} %bitcast.14, bf16[16,128,128]{2,1,0:T(8,128)(2,1)} %f_ref.1), custom_call_target="tpu_custom_call" | custom-call | tf_op jit(solution)/shard_map/pallas_call | solution.py:358
  140.2 1.1 copy.11
  141.3 1.0 bitcast_select_fusion
  (3 shorter events, 0.0 us)
Async XLA Ops:
  0.0 0.7 copy-start.3
  0.8 0.7 copy-start.2
  1.4 0.7 copy-start.1
  3.7 1.0 copy-start

commit v2 on v1

v2 whole, which is shorter than its diff:
```python
import jax
import jax.numpy as jnp
from jax import lax
from jax.experimental import pallas as pl
from jax.experimental.pallas import tpu as pltpu
from jax.sharding import PartitionSpec as P

VB = 64
MESH = pl.DeviceIdType.MESH
N_SEMS = 160


def kernel(
    virt, occ, pair, t_ref, ft_ref, f_ref, out_ref,
    t_own, t_all, fca, fdb, ht, rp, ra1, ra2, rb1, rb2, rc1, rc2, fin, fin_in,
    send, recv,
):
    row, col = lax.axis_index("row"), lax.axis_index("col")
    xh, y, k = row // 8, (row // 2) % 4, row % 2
    xl, z = col // 8, col % 8
    x = xh * 2 + xl

    def dev(x_to, y_to, z_to, k_to):
        return {"row": (x_to // 2) * 8 + y_to * 2 + k_to, "col": (x_to % 2) * 8 + z_to}

    def wrap(v, n):
        return lax.rem(v + n, n)

    xs = {s: wrap(x + s, 4) for s in (-1, 0, 1, 2)}
    ys = {s: wrap(y + s, 4) for s in (-1, 0, 1, 2)}
    zs = {s: wrap(z + s, 8) for s in range(-4, 5)}
    near = {
        "x": {s: dev(xs[s], y, z, k) for s in (-1, 1)},
        "y": {s: dev(x, ys[s], z, k) for s in (-1, 1)},
        "z": {s: dev(x, y, zs[s], k) for s in (-1, 1)},
    }
    sibling = dev(x, y, z, 1 - k)
    partner = dev(xh * 2 + k, y, z, xl)
    swapped = xl != k
    home = xl == k

    count = [0]
    pending = []

    def when(condition, action):
        if condition is None:
            action()
        else:
            pl.when(condition)(action)

    def put(src, dst, device, condition=None):
        number = count[0]
        count[0] += 1
        copy = pltpu.make_async_remote_copy(
            src_ref=src, dst_ref=dst, send_sem=send.at[number], recv_sem=recv.at[number],
            device_id=device, device_id_type=MESH,
        )
        when(condition, copy.start)
        pending.append((condition, copy))
        return copy

    def sign_of(label):
        return (1 - 2 * lax.rem(label, 2)).astype(jnp.float32)

    def two(block):
        low = lax.broadcasted_iota(jnp.int32, (1, 128), 1) < VB
        return jnp.where(low, sign_of(virt[2 * block]), sign_of(virt[2 * block + 1]))

    def two_rows(block):
        low = lax.broadcasted_iota(jnp.int32, (128, 1), 0) < VB
        return jnp.where(low, sign_of(virt[2 * block]), sign_of(virt[2 * block + 1]))

    pair_sign = [sign_of(occ[pair[2 * p]] + occ[pair[2 * p + 1]]) for p in range(8)]

    def mask(p):
        return 0.5 + 0.5 * (two_rows(col) * (two(row) * pair_sign[p]))

    barrier = pltpu.get_barrier_semaphore()
    for target in [*near["x"].values(), *near["y"].values(), *near["z"].values(), sibling]:
        pl.semaphore_signal(barrier, inc=1, device_id=target, device_id_type=MESH)

    for p in range(8):
        at = slice(p * 128, p * 128 + 128)
        t_own[:, at] = (t_ref[:, at].astype(jnp.float32) * mask(p)).astype(jnp.bfloat16)

    @pl.when(swapped)
    def _():
        pl.semaphore_signal(barrier, inc=1, device_id=partner, device_id_type=MESH)
        pl.semaphore_wait(barrier, 8)

    @pl.when(jnp.logical_not(swapped))
    def _():
        pl.semaphore_wait(barrier, 7)

    moves = []
    for src, dst in ((t_own, t_all.at[col]), (f_ref, fca.at[col])):
        number = count[0]
        count[0] += 1
        far = pltpu.make_async_remote_copy(
            src_ref=src, dst_ref=dst, send_sem=send.at[number], recv_sem=recv.at[number],
            device_id=partner, device_id_type=MESH,
        )
        near_copy = pltpu.make_async_copy(src, dst, recv.at[number])
        moves.append((far, near_copy))

    def own_start(i):
        far, near_copy = moves[i]

        @pl.when(swapped)
        def _():
            far.start()

        @pl.when(jnp.logical_not(swapped))
        def _():
            near_copy.start()

    def own_here(i):
        far, near_copy = moves[i]

        @pl.when(swapped)
        def _():
            far.wait_recv()

        @pl.when(jnp.logical_not(swapped))
        def _():
            near_copy.wait()

    ring_wait = {}
    side_wait = {}

    def part(name, shard, half):
        buf = t_all if name == "t" else fca
        at = k * 8 + shard
        rows = buf.shape[1]
        if half is None:
            return buf.at[at]
        return buf.at[at, pl.ds(half * (rows // 2), rows // 2)]

    def side_send(name, step):
        for sign in (1, -1) if step % 4 else (1,):
            piece = part(name, zs[-sign * step], None)
            side_wait[name, step, sign] = put(piece, piece, sibling)

    def side_done(name, step):
        for sign in (1, -1) if step % 4 else (1,):
            side_wait[name, step, sign].wait_recv()

    def t_send(step):
        for sign in (1, -1):
            piece = part("t", zs[-sign * (step - 1)], None if step < 4 else (1 - sign) // 2)
            ring_wait["t", step, sign] = put(piece, piece, near["z"][sign])

    def t_step(step):
        for sign in (1, -1):
            ring_wait["t", step, sign].wait_recv()
        if step < 4:
            t_send(step + 1)
        side_send("t", step)

    def t_done():
        for step in range(5):
            side_done("t", step)

    def f_send(step, half):
        for sign in (1, -1):
            if step < 4 or half == (1 - sign) // 2:
                piece = part("f", zs[-sign * (step - 1)], half)
                ring_wait["f", step, sign, half] = put(piece, piece, near["z"][sign])

    def f_step(step, half):
        for sign in (1, -1):
            if step < 4 or half == (1 - sign) // 2:
                ring_wait["f", step, sign, half].wait_recv()
        if step < 4:
            f_send(step + 1, half)
        if half == 1:
            side_send("f", step)

    def unit(xh_of, y_of, start, size):
        return fdb.at[xh_of, y_of, :, pl.ds(start, size)]

    def both_ways(piece, axis, condition=None):
        return {sign: put(piece, piece, near[axis][sign], condition) for sign in (1, -1)}

    lines = [jnp.where(home, xh, xs[-1] // 2), jnp.where(home, 1 - xh, xs[1] // 2)]
    sides = {1: xs[-1] // 2, -1: xs[1] // 2}
    moved = {}

    def wait(key, condition=None):
        for sign in (1, -1):
            when(condition, moved[key][sign].wait_recv)

    def a_start(s):
        own = unit(xh, y, 4 * s, 4)
        moved["ax", s] = both_ways(own, "x", home)

    def a_along(s, i, condition=None):
        piece = unit(lines[i], y, 4 * s, 4)
        return both_ways(piece, "y", condition)

    def b_start(s):
        own = unit(xh, y, 8 + 4 * s, 4)
        moved["by", s] = both_ways(own, "y", home)
        b_along(s, 0)

    def b_along(s, j):
        piece = unit(xh, ys[(0, -1, 1, 2)[j]], 8 + 4 * s, 4)
        moved["bx", s, j] = both_ways(piece, "x", home)

    def a_x(s):
        wait(("ax", s), swapped)
        moved["ax2", s] = {
            sign: put(piece, piece, near["x"][sign], swapped)
            for sign in (1, -1)
            for piece in [unit(sides[sign], y, 4 * s + 1 - sign, 2)]
        }
        moved["ay", s, 0] = a_along(s, 0)

    def a_x2(s):
        wait(("ax2", s), home)
        moved["ay", s, 1] = a_along(s, 1)

    def a_y(s, i):
        wait(("ay", s, i))
        moved["ay2", s, i] = {
            sign: put(piece, piece, near["y"][sign])
            for sign in (1, -1)
            for piece in [unit(lines[i], ys[-sign], 4 * s + 1 - sign, 2)]
        }

    def b_y(s):
        wait(("by", s), home)
        moved["by2", s] = {
            sign: put(piece, piece, near["y"][sign], home)
            for sign in (1, -1)
            for piece in [unit(xh, ys[-sign], 8 + 4 * s + 1 - sign, 2)]
        }
        b_along(s, 1)
        b_along(s, 2)

    def b_y2(s):
        wait(("by2", s), home)
        b_along(s, 3)

    def b_x(s, j):
        wait(("bx", s, j), swapped)
        moved["bx2", s, j] = {
            sign: put(piece, piece, near["x"][sign], swapped)
            for sign in (1, -1)
            for piece in [unit(sides[sign], ys[(0, -1, 1, 2)[j]], 8 + 4 * s + 1 - sign, 2)]
        }

    def a_done(s):
        for i in (0, 1):
            wait(("ay2", s, i))

    def b_done(s):
        for j in range(4):
            wait(("bx2", s, j), home)

    given = put(ft_ref, fdb.at[xh, y, k], sibling, swapped)
    kept = pltpu.make_async_copy(ft_ref, fdb.at[xh, y, k], send.at[N_SEMS - 1])
    pl.when(home)(kept.start)

    def plane_own():
        pl.when(home)(given.wait_recv)
        pl.when(home)(kept.wait)

    def stage1(first_q):
        def body(n, _):
            lhs = jnp.concatenate(
                [
                    fdb[r // 8, (r // 2) % 4, r % 2, first_q : first_q + 4].reshape(512, 128)
                    for r in range(16)
                ],
                axis=1,
            )
            rhs = t_all[:, :, pl.ds(pl.multiple_of(n * 256, 256), 256)].reshape(2048, 256)
            out = jnp.dot(lhs, rhs, preferred_element_type=jnp.float32).astype(jnp.bfloat16)
            for i in range(2):
                rows = pl.ds(pl.multiple_of(n * 256 + i * 128, 128), 128)
                for j in range(4):
                    at = (first_q + j) * 128
                    ht[rows, at : at + 128] = out[j * 128 : j * 128 + 128, i * 128 : i * 128 + 128]
            return 0

        lax.fori_loop(0, 4, body, 0)

    def stage2(lo, hi):
        for step in sorted({(n + 1) // 2 for n in range(lo, hi)}):
            side_done("f", step)

        def body(n, _):
            away = (n + 1) // 2
            shard = wrap(z + jnp.where(lax.rem(n, 2) == 1, away, 8 - away), 8)
            rhs = jnp.concatenate(
                [fca[shard].reshape(2048, 128), fca[8 + shard].reshape(2048, 128)], axis=1
            )
            out = jnp.dot(ht[...], rhs, preferred_element_type=jnp.float32).astype(jnp.bfloat16)
            rp[0, shard // 2, lax.rem(shard, 2)] = out[:, :128]
            rp[1, shard // 2, lax.rem(shard, 2)] = out[:, 128:]
            return 0

        lax.fori_loop(lo, hi, body, 0)

    def strip(half, v, start, size):
        if half == 0:
            return (slice(None), v, slice(None), pl.ds(start, size))
        return (v // 2, slice(None), v % 2, pl.ds(start, size))

    sums1, sums2, last1, last2, alone1, alone2, back = {}, {}, {}, {}, {}, {}, {}
    got1, got2 = {0: ra1, 1: rb1}, {0: ra2, 1: rb2}
    scatter = {0: ("y", "x", ys, xs), 1: ("x", "y", xs, ys)}

    def slot(sign):
        return (1 - sign) // 2

    def quarter(half, sign):
        return half * 512 + slot(sign) * 256

    def one(half, u):
        return (u // 2, y, u % 2) if half == 0 else (x // 2, u, x % 2)

    def f32(v):
        return v.astype(jnp.float32)

    def sum_first(half):
        axis, _, vs, _ = scatter[half]
        for sign in (1, -1):
            src = rp.at[strip(half, vs[2], quarter(half, sign), 256)]
            sums1[half, sign] = put(src, got1[half].at[slot(sign)], near[axis][sign])
        for sign in (1, -1):
            src = rp.at[strip(half, vs[sign], quarter(half, -sign), 256)]
            dst = got2[half].at[slot(sign), slot(-sign)]
            alone1[half, sign] = put(src, dst, near[axis][sign])

    def sum_second(half):
        axis, _, vs, _ = scatter[half]
        for sign in (1, -1):
            sums1[half, sign].wait_recv()
            at = strip(half, vs[sign], quarter(half, sign), 256)
            rp[at] = (f32(rp[at]) + f32(got1[half][slot(sign)])).astype(jnp.bfloat16)
            dst = got2[half].at[slot(sign), slot(sign)]
            sums2[half, sign] = put(rp.at[at], dst, near[axis][sign])

    def line_sum(half, u, i):
        at = (*one(half, u), pl.ds(half * 512 + i * 256, 256))
        got = got2[half]
        if half == 0:
            a, b = got[0, i, u // 2, u % 2], got[1, i, u // 2, u % 2]
        else:
            a, b = got[0, i, u], got[1, i, u]
        rp[at] = (f32(rp[at]) + f32(a) + f32(b)).astype(jnp.bfloat16)
        return rp.at[at]

    def sum_third(half):
        _, axis, _, us = scatter[half]
        for sign in (1, -1):
            alone1[half, sign].wait_recv()
        for sign in (1, -1):
            sums2[half, sign].wait_recv()
        for sign in (1, -1):
            src = line_sum(half, us[2], slot(sign))
            last1[half, sign] = put(src, rc1.at[half, slot(sign)], near[axis][sign])
        for sign in (1, -1):
            src = line_sum(half, us[sign], slot(-sign))
            alone2[half, sign] = put(src, rc2.at[half, slot(sign), slot(-sign)], near[axis][sign])
        for sign in (1, -1):
            line_sum(half, us[sign], slot(sign))
            line_sum(half, us[0], slot(sign))

    def sum_fourth(half):
        _, axis, _, us = scatter[half]
        for sign in (1, -1):
            last1[half, sign].wait_recv()
            at = (*one(half, us[sign]), pl.ds(quarter(half, sign), 256))
            rp[at] = (f32(rp[at]) + f32(rc1[half, slot(sign)])).astype(jnp.bfloat16)
            dst = rc2.at[half, slot(sign), slot(sign)]
            last2[half, sign] = put(rp.at[at], dst, near[axis][sign])

    def sum_last(half):
        _, _, _, us = scatter[half]
        for sign in (1, -1):
            alone2[half, sign].wait_recv()
        for sign in (1, -1):
            last2[half, sign].wait_recv()
        for i in (0, 1):
            rows = pl.ds(half * 512 + i * 256, 256)
            mine = f32(rp[(*one(half, us[0]), rows)])
            fin[rows, :] = (mine + f32(rc2[half, 0, i]) + f32(rc2[half, 1, i])).astype(jnp.bfloat16)
        rows = pl.ds(half * 512, 512)
        back[half] = put(fin.at[rows], fin_in.at[rows], partner, swapped)

    def give(half):
        def write(result):
            for p in range(half * 4, half * 4 + 4):
                rows = slice(p * 128, p * 128 + 128)
                out_ref[rows, :] = (f32(result[rows, :]) * mask(p)).astype(jnp.bfloat16)

        @pl.when(swapped)
        def _():
            back[half].wait_recv()
            write(fin_in)

        pl.when(home)(lambda: write(fin))

    own_start(0)
    own_start(1)
    own_here(0)
    t_send(1)
    plane_own()
    own_here(1)
    f_send(1, 0)
    a_start(0)
    a_x(0)
    b_start(0)
    a_start(1)
    b_y(0)
    t_step(1)
    b_start(1)
    b_y2(0)
    f_send(1, 1)
    t_step(2)
    a_x(1)
    b_y(1)
    a_y(1, 0)
    f_step(1, 0)
    side_send("t", 0)
    a_x2(1)
    b_x(0, 1)
    t_step(3)
    b_x(0, 3)
    b_x(0, 2)
    a_x2(0)
    f_step(1, 1)
    a_y(1, 1)
    f_step(2, 0)
    b_y2(1)
    a_y(0, 0)
    t_step(4)
    b_x(0, 0)
    b_x(1, 1)
    side_send("f", 0)
    a_y(0, 1)
    b_x(1, 2)
    b_x(1, 0)
    f_step(2, 1)
    t_done()
    b_done(0)
    stage1(8)
    b_x(1, 3)
    a_done(1)
    stage1(4)
    a_done(0)
    stage1(0)
    b_done(1)
    stage1(12)
    f_step(3, 0)
    f_step(3, 1)
    stage2(3, 5)
    stage2(0, 3)
    f_step(4, 0)
    f_step(4, 1)
    stage2(5, 7)
    stage2(7, 8)

    def both(step):
        step(0)
        step(1)

    both(sum_first)
    both(sum_second)
    both(sum_third)
    both(sum_fourth)
    both(sum_last)
    both(give)

    @pl.when(swapped)
    def _():
        for far, _ in moves:
            far.wait_send()

    for condition, copy in pending:
        when(condition, copy.wait_send)


def ladder(virt, occ, pair, t, ft, f):
    bf16 = jnp.bfloat16
    hbm, vmem = pl.BlockSpec(memory_space=pl.ANY), pl.BlockSpec(memory_space=pltpu.VMEM)
    smem = pl.BlockSpec(memory_space=pltpu.SMEM)
    return pl.pallas_call(
        kernel,
        out_shape=jax.ShapeDtypeStruct((1024, 128), bf16),
        in_specs=[smem, smem, smem, vmem, hbm, hbm],
        out_specs=vmem,
        scratch_shapes=[
            pltpu.VMEM((128, 1024), bf16),
            pltpu.VMEM((16, 128, 1024), bf16),
            pltpu.VMEM((16, 16, 128, 128), bf16),
            pltpu.VMEM((2, 4, 2, 16, 128, 128), bf16),
            pltpu.VMEM((1024, 2048), bf16),
            pltpu.VMEM((2, 4, 2, 1024, 128), bf16),
            pltpu.VMEM((2, 2, 2, 256, 128), bf16),
            pltpu.VMEM((2, 2, 2, 2, 256, 128), bf16),
            pltpu.VMEM((2, 4, 256, 128), bf16),
            pltpu.VMEM((2, 2, 4, 256, 128), bf16),
            pltpu.VMEM((2, 2, 256, 128), bf16),
            pltpu.VMEM((2, 2, 2, 256, 128), bf16),
            pltpu.VMEM((1024, 128), bf16),
            pltpu.VMEM((1024, 128), bf16),
            pltpu.SemaphoreType.DMA((N_SEMS,)),
            pltpu.SemaphoreType.DMA((N_SEMS,)),
        ],
        compiler_params=pltpu.CompilerParams(
            collective_id=0, has_side_effects=True, vmem_limit_bytes=56 * 1024 * 1024
        ),
    )(virt, occ, pair, t, ft, f)


def on_device(amplitudes, factors, virt_irrep, occupied_symmetry_label, pair_index):
    rows, pairs, width = amplitudes.shape
    t = amplitudes.transpose(2, 1, 0).reshape(width, pairs * rows)
    ft = factors.transpose(0, 2, 1)
    pair = pair_index.reshape(pairs * 2)
    out = ladder(virt_irrep, occupied_symmetry_label, pair, t, ft, factors)
    return out.reshape(pairs, width, rows).transpose(2, 0, 1)


def solution(mesh):
    in_specs = (P("row", None, "col"), P(None, "row", "col"), P(), P(), P())
    out_specs = P("row", None, "col")
    return jax.shard_map(
        on_device, mesh=mesh, in_specs=in_specs, out_specs=out_specs, check_vma=False
    )
```

time: 143 us -> 129 us (0.902)
  Pallas kernels: 134 us -> 122 us
  other arithmetic: 2.73 us -> 0 us
    pallas_call x1, Pallas kernels: 134 us -> 122 us  [ladder(): pl.pallas_call(kernel, out_shape=jax.ShapeDtypeStruct((1024, 128), bf16),...]
    unnamed x10 -> x7, local copies, waits for them, and re-layouts: 3.8 us -> 2.51 us
where the time goes in v2:
time: 129 us; the launch traced here: 128 us
  Pallas kernels  122 us (95%)
  local copies, waits for them, and re-layouts  6.21 us (5%)
    pallas_call x1, Pallas kernels, ladder(): pl.pallas_call(kernel, out_shape=jax.ShapeDtypeStruct((1024, 128), bf16),...  122 us

profile of v2, /device:TPU:1, one launch (start us, length us, event | category | flops | bytes accessed | tf_op | source)
XLA Modules:
  0.0 128.4 jit_solution(1587236877209820133)
XLA Ops:
  0.0 0.0 copy-start.1
  0.0 0.7 copy-done.1
  0.7 0.1 copy.10
  0.8 0.6 reshape.9.pair
  1.4 0.0 copy-start
  1.4 1.3 copy.11
  2.6 0.8 copy.16
  3.4 0.0 copy-done
  3.4 1.0 copy.12
  4.4 122.2 %shard_map.55 = bf16[1024,128]{1,0:T(8,128)(2,1)} custom-call(s32[32]{0:T(128)} %virt.1, s32[200]{0:T(256)} %occ.1, s32[16]{0:T(128)} %reshape.9.pair, bf16[128,1024]{1,0:T(8,128)(2,1)} %bitcast.10, bf16[16,128,128]{2,1,0:T(8,128)(2,1)} %bitcast.8, bf16[16,128,128]{2,1,0:T(8,128)(2,1)} %f_ref.1), custom_call_target="tpu_custom_call" | custom-call | tf_op jit(solution)/shard_map/pallas_call | solution.py:491
  126.6 1.8 %copy.13 = bf16[8,128,128]{1,0,2:T(8,128)(2,1)} copy(bf16[8,128,128]{2,1,0:T(8,128)(2,1)} %bitcast.11) | data formatting | bytes 524288 | tf_op jit(solution)/shard_map/reshape | solution.py:526
Async XLA Ops:
  0.0 0.7 copy-start.1
  1.4 2.0 %copy-start = (bf16[16,128,128]{2,1,0:T(8,128)(2,1)S(1)}, bf16[16,128,128]{2,1,0:T(8,128)(2,1)}, u32[]{:S(2)}) copy-start(bf16[16,128,128]{2,1,0:T(8,128)(2,1)} %f_ref.1) | copy-start | bytes 1572868

commit v3 on v2

--- a/solution.py
+++ b/solution.py
@@ -7,12 +7,12 @@
 
 VB = 64
 MESH = pl.DeviceIdType.MESH
-N_SEMS = 160
+N_SEMS = 190
 
 
 def kernel(
     virt, occ, pair, t_ref, ft_ref, f_ref, out_ref,
-    t_own, t_all, fca, fdb, ht, rp, ra1, ra2, rb1, rb2, rc1, rc2, fin, fin_in,
+    t_own, t_all, fca, fdb, ht, rp, ra1, ra2, rb1, rb2, rc1, rc2, own_in,
     send, recv,
 ):
     row, col = lax.axis_index("row"), lax.axis_index("col")
@@ -38,6 +38,11 @@
     partner = dev(xh * 2 + k, y, z, xl)
     swapped = xl != k
     home = xl == k
+    owner = {
+        "x": {s: dev((xs[s] // 2) * 2 + k, y, z, xs[s] % 2) for s in (-1, 1)},
+        "y": {s: dev(xh * 2 + k, ys[s], z, xl) for s in (-1, 1)},
+    }
+    across_chip = dev(xs[2], y, z, 1 - k)
 
     count = [0]
     pending = []
@@ -70,13 +75,13 @@
         low = lax.broadcasted_iota(jnp.int32, (128, 1), 0) < VB
         return jnp.where(low, sign_of(virt[2 * block]), sign_of(virt[2 * block + 1]))
 
-    pair_sign = [sign_of(occ[pair[2 * p]] + occ[pair[2 * p + 1]]) for p in range(8)]
+    pair_sign = [sign_of(occ[pair[p, 0]] + occ[pair[p, 1]]) for p in range(8)]
 
     def mask(p):
         return 0.5 + 0.5 * (two_rows(col) * (two(row) * pair_sign[p]))
 
     barrier = pltpu.get_barrier_semaphore()
-    for target in [*near["x"].values(), *near["y"].values(), *near["z"].values(), sibling]:
+    for target in [*near["x"].values(), *near["y"].values(), *near["z"].values(), sibling, across_chip]:
         pl.semaphore_signal(barrier, inc=1, device_id=target, device_id_type=MESH)
 
     for p in range(8):
@@ -85,12 +90,13 @@
 
     @pl.when(swapped)
     def _():
-        pl.semaphore_signal(barrier, inc=1, device_id=partner, device_id_type=MESH)
-        pl.semaphore_wait(barrier, 8)
+        for target in [partner, *owner["y"].values()]:
+            pl.semaphore_signal(barrier, inc=1, device_id=target, device_id_type=MESH)
+        pl.semaphore_wait(barrier, 11)
 
     @pl.when(jnp.logical_not(swapped))
     def _():
-        pl.semaphore_wait(barrier, 7)
+        pl.semaphore_wait(barrier, 8)
 
     moves = []
     for src, dst in ((t_own, t_all.at[col]), (f_ref, fca.at[col])):
@@ -310,7 +316,6 @@
 
     sums1, sums2, last1, last2, alone1, alone2, back = {}, {}, {}, {}, {}, {}, {}
     got1, got2 = {0: ra1, 1: rb1}, {0: ra2, 1: rb2}
-    scatter = {0: ("y", "x", ys, xs), 1: ("x", "y", xs, ys)}
 
     def slot(sign):
         return (1 - sign) // 2
@@ -324,24 +329,57 @@
     def f32(v):
         return v.astype(jnp.float32)
 
-    def sum_first(half):
-        axis, _, vs, _ = scatter[half]
-        for sign in (1, -1):
-            src = rp.at[strip(half, vs[2], quarter(half, sign), 256)]
-            sums1[half, sign] = put(src, got1[half].at[slot(sign)], near[axis][sign])
-        for sign in (1, -1):
-            src = rp.at[strip(half, vs[sign], quarter(half, -sign), 256)]
-            dst = got2[half].at[slot(sign), slot(-sign)]
-            alone1[half, sign] = put(src, dst, near[axis][sign])
-
-    def sum_second(half):
-        axis, _, vs, _ = scatter[half]
-        for sign in (1, -1):
-            sums1[half, sign].wait_recv()
-            at = strip(half, vs[sign], quarter(half, sign), 256)
-            rp[at] = (f32(rp[at]) + f32(got1[half][slot(sign)])).astype(jnp.bfloat16)
-            dst = got2[half].at[slot(sign), slot(sign)]
-            sums2[half, sign] = put(rp.at[at], dst, near[axis][sign])
+    odd = lax.rem(z, 2) == 1
+    group_y = [wrap(z // 2 + jnp.where(odd, s, (-s) % 4), 4) for s in (0, 1, 3, 2)]
+
+    def later(src, dst, device):
+        number = count[0]
+        count[0] += 1
+        copy = pltpu.make_async_remote_copy(
+            src_ref=src, dst_ref=dst, send_sem=send.at[number], recv_sem=recv.at[number],
+            device_id=device, device_id_type=MESH,
+        )
+        pending.append((None, copy))
+        return copy
+
+    for sign in (1, -1):
+        src = rp.at[strip(0, ys[2], quarter(0, sign), 256)]
+        sums1[0, sign] = later(src, ra1.at[slot(sign)], near["y"][sign])
+        src = rp.at[strip(0, ys[sign], quarter(0, -sign), 256)]
+        alone1[0, sign] = later(src, ra2.at[slot(sign), slot(-sign)], near["y"][sign])
+        src = rp.at[(*one(1, ys[2]), pl.ds(quarter(1, sign), 256))]
+        last1[1, sign] = later(src, rc1.at[1, slot(sign)], near["y"][sign])
+        src = rp.at[(*one(1, ys[sign]), pl.ds(quarter(1, -sign), 256))]
+        alone2[1, sign] = later(src, rc2.at[1, slot(sign), slot(-sign)], owner["y"][sign])
+
+    def by_part(g, far, next_to):
+        away = wrap(group_y[g] - y, 4)
+
+        @pl.when(away == 2)
+        def _():
+            far[1].start()
+            far[-1].start()
+
+        pl.when(away == 1)(next_to[1].start)
+        pl.when(away == 3)(next_to[-1].start)
+
+    def group_send(g):
+        by_part(g, {s: sums1[0, s] for s in (1, -1)}, {s: alone1[0, s] for s in (1, -1)})
+        for sign in (1, -1):
+            src = rp.at[xs[2] // 2, group_y[g], xs[2] % 2, pl.ds(quarter(1, sign), 256)]
+            sums1[1, g, sign] = put(src, rb1.at[slot(sign), group_y[g]], near["x"][sign])
+        for sign in (1, -1):
+            src = rp.at[xs[sign] // 2, group_y[g], xs[sign] % 2, pl.ds(quarter(1, -sign), 256)]
+            dst = rb2.at[slot(sign), slot(-sign), group_y[g]]
+            alone1[1, g, sign] = put(src, dst, near["x"][sign])
+
+    def b_sum(g):
+        for sign in (1, -1):
+            sums1[1, g, sign].wait_recv()
+            at = (xs[sign] // 2, group_y[g], xs[sign] % 2, pl.ds(quarter(1, sign), 256))
+            rp[at] = (f32(rp[at]) + f32(rb1[slot(sign), group_y[g]])).astype(jnp.bfloat16)
+            dst = rb2.at[slot(sign), slot(sign), group_y[g]]
+            sums2[1, g, sign] = put(rp.at[at], dst, near["x"][sign])
 
     def line_sum(half, u, i):
         at = (*one(half, u), pl.ds(half * 512 + i * 256, 256))
@@ -353,127 +391,147 @@
         rp[at] = (f32(rp[at]) + f32(a) + f32(b)).astype(jnp.bfloat16)
         return rp.at[at]
 
-    def sum_third(half):
-        _, axis, _, us = scatter[half]
-        for sign in (1, -1):
-            alone1[half, sign].wait_recv()
-        for sign in (1, -1):
-            sums2[half, sign].wait_recv()
-        for sign in (1, -1):
-            src = line_sum(half, us[2], slot(sign))
-            last1[half, sign] = put(src, rc1.at[half, slot(sign)], near[axis][sign])
-        for sign in (1, -1):
-            src = line_sum(half, us[sign], slot(-sign))
-            alone2[half, sign] = put(src, rc2.at[half, slot(sign), slot(-sign)], near[axis][sign])
-        for sign in (1, -1):
-            line_sum(half, us[sign], slot(sign))
-            line_sum(half, us[0], slot(sign))
+    def b_line(g):
+        for sign in (1, -1):
+            alone1[1, g, sign].wait_recv()
+            sums2[1, g, sign].wait_recv()
+        for i in (0, 1):
+            line_sum(1, group_y[g], i)
+        by_part(g, {s: last1[1, s] for s in (1, -1)}, {s: alone2[1, s] for s in (1, -1)})
+
+    def a_sum():
+        for sign in (1, -1):
+            sums1[0, sign].wait_recv()
+            at = strip(0, ys[sign], quarter(0, sign), 256)
+            rp[at] = (f32(rp[at]) + f32(ra1[slot(sign)])).astype(jnp.bfloat16)
+            sums2[0, sign] = put(rp.at[at], ra2.at[slot(sign), slot(sign)], near["y"][sign])
+
+    def a_line():
+        for sign in (1, -1):
+            alone1[0, sign].wait_recv()
+            sums2[0, sign].wait_recv()
+        for sign in (1, -1):
+            src = line_sum(0, xs[2], slot(sign))
+            last1[0, sign] = put(src, rc1.at[0, slot(sign)], near["x"][sign])
+        for sign in (1, -1):
+            src = line_sum(0, xs[sign], slot(-sign))
+            alone2[0, sign] = put(src, rc2.at[0, slot(sign), slot(-sign)], owner["x"][sign])
+        for sign in (1, -1):
+            line_sum(0, xs[0], slot(sign))
+        own_send(0)
+        for sign in (1, -1):
+            line_sum(0, xs[sign], slot(sign))
 
     def sum_fourth(half):
-        _, axis, _, us = scatter[half]
+        axis, us = (("x", xs), ("y", ys))[half]
         for sign in (1, -1):
             last1[half, sign].wait_recv()
             at = (*one(half, us[sign]), pl.ds(quarter(half, sign), 256))
             rp[at] = (f32(rp[at]) + f32(rc1[half, slot(sign)])).astype(jnp.bfloat16)
             dst = rc2.at[half, slot(sign), slot(sign)]
-            last2[half, sign] = put(rp.at[at], dst, near[axis][sign])
+            last2[half, sign] = put(rp.at[at], dst, owner[axis][sign])
+
+    def own_send(half):
+        rows = pl.ds(half * 512, 512)
+        back[half] = put(rp.at[x // 2, y, x % 2, rows], own_in.at[rows], partner, swapped)
 
     def sum_last(half):
-        _, _, _, us = scatter[half]
         for sign in (1, -1):
             alone2[half, sign].wait_recv()
-        for sign in (1, -1):
             last2[half, sign].wait_recv()
-        for i in (0, 1):
-            rows = pl.ds(half * 512 + i * 256, 256)
-            mine = f32(rp[(*one(half, us[0]), rows)])
-            fin[rows, :] = (mine + f32(rc2[half, 0, i]) + f32(rc2[half, 1, i])).astype(jnp.bfloat16)
-        rows = pl.ds(half * 512, 512)
-        back[half] = put(fin.at[rows], fin_in.at[rows], partner, swapped)
-
-    def give(half):
-        def write(result):
+
+        def write(own):
             for p in range(half * 4, half * 4 + 4):
                 rows = slice(p * 128, p * 128 + 128)
-                out_ref[rows, :] = (f32(result[rows, :]) * mask(p)).astype(jnp.bfloat16)
+                i, got = (p % 4) // 2, slice((p % 2) * 128, (p % 2) * 128 + 128)
+                total = f32(own(rows)) + f32(rc2[half, 0, i, got]) + f32(rc2[half, 1, i, got])
+                out_ref[rows, :] = (total * mask(p)).astype(jnp.bfloat16)
 
         @pl.when(swapped)
         def _():
             back[half].wait_recv()
-            write(fin_in)
-
-        pl.when(home)(lambda: write(fin))
+            write(lambda rows: own_in[rows, :])
+
+        pl.when(home)(lambda: write(lambda rows: rp[x // 2, y, x % 2, rows, :]))
 
     own_start(0)
-    own_start(1)
     own_here(0)
     t_send(1)
     plane_own()
+    own_start(1)
+    t_step(1)
+    a_start(1)
+    b_start(1)
     own_here(1)
+    a_x(1)
     f_send(1, 0)
-    a_start(0)
-    a_x(0)
-    b_start(0)
-    a_start(1)
-    b_y(0)
-    t_step(1)
-    b_start(1)
-    b_y2(0)
-    f_send(1, 1)
-    t_step(2)
-    a_x(1)
     b_y(1)
     a_y(1, 0)
+    b_start(0)
+    f_send(1, 1)
+    side_send("t", 0)
+    t_step(2)
+    b_y2(1)
     f_step(1, 0)
-    side_send("t", 0)
     a_x2(1)
+    side_send("f", 0)
+    a_start(0)
+    b_x(1, 3)
+    a_x(0)
+    t_step(3)
+    b_y(0)
+    b_y2(0)
+    b_x(1, 1)
+    a_y(1, 1)
+    f_step(1, 1)
+    b_x(1, 2)
+    a_y(0, 0)
+    f_step(2, 0)
+    a_done(1)
     b_x(0, 1)
-    t_step(3)
+    t_step(4)
+    t_done()
+    a_x2(0)
+    b_x(1, 0)
+    b_x(0, 2)
+    stage1(4)
+    b_x(0, 0)
     b_x(0, 3)
-    b_x(0, 2)
-    a_x2(0)
-    f_step(1, 1)
-    a_y(1, 1)
-    f_step(2, 0)
-    b_y2(1)
-    a_y(0, 0)
-    t_step(4)
-    b_x(0, 0)
-    b_x(1, 1)
-    side_send("f", 0)
-    a_y(0, 1)
-    b_x(1, 2)
-    b_x(1, 0)
     f_step(2, 1)
-    t_done()
-    b_done(0)
-    stage1(8)
-    b_x(1, 3)
-    a_done(1)
-    stage1(4)
-    a_done(0)
-    stage1(0)
     b_done(1)
     stage1(12)
+    b_done(0)
+    a_y(0, 1)
+    stage1(8)
+    a_done(0)
     f_step(3, 0)
     f_step(3, 1)
+    stage1(0)
+    stage2(0, 3)
+    group_send(0)
     stage2(3, 5)
-    stage2(0, 3)
+    group_send(1)
+    b_sum(0)
     f_step(4, 0)
     f_step(4, 1)
     stage2(5, 7)
+    group_send(2)
+    b_sum(1)
     stage2(7, 8)
-
-    def both(step):
-        step(0)
-        step(1)
-
-    both(sum_first)
-    both(sum_second)
-    both(sum_third)
-    both(sum_fourth)
-    both(sum_last)
-    both(give)
+    group_send(3)
+    b_sum(2)
+    b_line(0)
+    b_sum(3)
+    b_line(1)
+    b_line(2)
+    a_sum()
+    b_line(3)
+    own_send(1)
+    a_line()
+    sum_fourth(1)
+    sum_fourth(0)
+    sum_last(1)
+    sum_last(0)
 
     @pl.when(swapped)
     def _():
@@ -507,7 +565,6 @@
             pltpu.VMEM((2, 2, 256, 128), bf16),
             pltpu.VMEM((2, 2, 2, 256, 128), bf16),
             pltpu.VMEM((1024, 128), bf16),
-            pltpu.VMEM((1024, 128), bf16),
             pltpu.SemaphoreType.DMA((N_SEMS,)),
             pltpu.SemaphoreType.DMA((N_SEMS,)),
         ],
@@ -521,8 +578,7 @@
     rows, pairs, width = amplitudes.shape
     t = amplitudes.transpose(2, 1, 0).reshape(width, pairs * rows)
     ft = factors.transpose(0, 2, 1)
-    pair = pair_index.reshape(pairs * 2)
-    out = ladder(virt_irrep, occupied_symmetry_label, pair, t, ft, factors)
+    out = ladder(virt_irrep, occupied_symmetry_label, pair_index, t, ft, factors)
     return out.reshape(pairs, width, rows).transpose(2, 0, 1)
 
 

time: 129 us -> 122 us (0.946)
  Pallas kernels: 122 us -> 116 us
    pallas_call x1, Pallas kernels: 122 us -> 116 us  [ladder(): pl.pallas_call(kernel, out_shape=jax.ShapeDtypeStruct((1024, 128), bf16),...]
where the time goes in v3:
time: 122 us
  Pallas kernels  116 us (95%)
  local copies, waits for them, and re-layouts  6.18 us (5%)
    pallas_call x1, Pallas kernels, ladder(): pl.pallas_call(kernel, out_shape=jax.ShapeDtypeStruct((1024, 128), bf16),...  116 us
    unnamed x7, local copies, waits for them, and re-layouts  3.1 us

profile of v3, /device:TPU:1, one launch (start us, length us, event | category | flops | bytes accessed | tf_op | source)
XLA Modules:
  0.0 122.0 jit_solution(8838954774049903024)
XLA Ops:
  0.0 0.0 copy-start.1
  0.0 0.7 copy-done.1
  0.7 0.7 copy.8.pair
  1.3 0.0 copy-start
  1.4 1.3 %copy.6 = bf16[128,8,128]{2,1,0:T(8,128)(2,1)S(1)} copy(bf16[128,8,128]{0,1,2:T(8,128)(2,1)} %bitcast.12) | data formatting | bytes 524288 | tf_op jit(solution)/shard_map/transpose | solution.py:579
  2.6 0.8 copy.12
  3.4 0.0 copy-done
  3.4 1.0 copy.7
  4.4 115.8 %shard_map.55 = bf16[1024,128]{1,0:T(8,128)(2,1)} custom-call(s32[32]{0:T(128)} %virt.1, s32[200]{0:T(256)} %occ.1, s32[8,2]{1,0:T(8,128)} %copy.8.pair, bf16[128,1024]{1,0:T(8,128)(2,1)} %bitcast.9, bf16[16,128,128]{2,1,0:T(8,128)(2,1)} %bitcast.8, bf16[16,128,128]{2,1,0:T(8,128)(2,1)} %f_ref.1), custom_call_target="tpu_custom_call" | custom-call | tf_op jit(solution)/shard_map/pallas_call | solution.py:549
  120.2 1.8 %copy.9 = bf16[8,128,128]{1,0,2:T(8,128)(2,1)} copy(bf16[8,128,128]{2,1,0:T(8,128)(2,1)} %bitcast.10) | data formatting | bytes 524288 | tf_op jit(solution)/shard_map/reshape | solution.py:582
Async XLA Ops:
  0.0 0.7 copy-start.1
  1.3 2.0 %copy-start = (bf16[16,128,128]{2,1,0:T(8,128)(2,1)S(1)}, bf16[16,128,128]{2,1,0:T(8,128)(2,1)}, u32[]{:S(2)}) copy-start(bf16[16,128,128]{2,1,0:T(8,128)(2,1)} %f_ref.1) | copy-start | bytes 1572868

commit v4 on v3

--- a/solution.py
+++ b/solution.py
@@ -75,7 +75,7 @@
         low = lax.broadcasted_iota(jnp.int32, (128, 1), 0) < VB
         return jnp.where(low, sign_of(virt[2 * block]), sign_of(virt[2 * block + 1]))
 
-    pair_sign = [sign_of(occ[pair[p, 0]] + occ[pair[p, 1]]) for p in range(8)]
+    pair_sign = [sign_of(occ[pair[0, p]] + occ[pair[1, p]]) for p in range(8)]
 
     def mask(p):
         return 0.5 + 0.5 * (two_rows(col) * (two(row) * pair_sign[p]))
@@ -86,7 +86,7 @@
 
     for p in range(8):
         at = slice(p * 128, p * 128 + 128)
-        t_own[:, at] = (t_ref[:, at].astype(jnp.float32) * mask(p)).astype(jnp.bfloat16)
+        t_own[:, at] = (t_ref[:, p, :].astype(jnp.float32) * mask(p)).astype(jnp.bfloat16)
 
     @pl.when(swapped)
     def _():
@@ -576,9 +576,9 @@
 
 def on_device(amplitudes, factors, virt_irrep, occupied_symmetry_label, pair_index):
     rows, pairs, width = amplitudes.shape
-    t = amplitudes.transpose(2, 1, 0).reshape(width, pairs * rows)
+    t = amplitudes.transpose(2, 1, 0)
     ft = factors.transpose(0, 2, 1)
-    out = ladder(virt_irrep, occupied_symmetry_label, pair_index, t, ft, factors)
+    out = ladder(virt_irrep, occupied_symmetry_label, pair_index.T, t, ft, factors)
     return out.reshape(pairs, width, rows).transpose(2, 0, 1)
 
 

time: 122 us -> 121 us (level)
  local copies, waits for them, and re-layouts: 6.18 us -> 4.78 us
    transpose x1 -> x0, local copies, waits for them, and re-layouts: 1.26 us -> none  [on_device(): t = amplitudes.transpose(2, 1, 0).reshape(width, pairs * rows)]
    unnamed x7 -> x4, local copies, waits for them, and re-layouts: 3.1 us -> 2.96 us
where the time goes in v4:
time: 121 us
  Pallas kernels  116 us (96%)
  local copies, waits for them, and re-layouts  4.78 us (4%)
    pallas_call x1, Pallas kernels, ladder(): pl.pallas_call(kernel, out_shape=jax.ShapeDtypeStruct((1024, 128), bf16),...  116 us
    unnamed x4, local copies, waits for them, and re-layouts  2.96 us

profile of v4, /device:TPU:1, one launch (start us, length us, event | category | flops | bytes accessed | tf_op | source)
XLA Modules:
  0.0 120.6 jit_solution(7014126119007503235)
XLA Ops:
  0.0 0.0 copy-start
  0.0 2.0 %copy.6 = bf16[128,8,128]{0,1,2:T(8,128)(2,1)} copy(bf16[128,8,128]{2,1,0:T(8,128)(2,1)} %param.5) | data formatting | bytes 524288 | tf_op args[0]
  2.0 0.0 copy-done
  2.0 1.0 copy.7
  3.0 115.8 %shard_map.55 = bf16[1024,128]{1,0:T(8,128)(2,1)} custom-call(s32[32]{0:T(128)} %virt.1, s32[200]{0:T(256)} %occ.1, s32[2,8]{1,0:T(2,128)} %bitcast.8, bf16[128,8,128]{2,1,0:T(8,128)(2,1)} %bitcast.7, bf16[16,128,128]{2,1,0:T(8,128)(2,1)} %bitcast.5, bf16[16,128,128]{2,1,0:T(8,128)(2,1)} %f_ref.1), custom_call_target="tpu_custom_call" | custom-call | tf_op jit(solution)/shard_map/pallas_call | solution.py:549
  118.8 1.8 %copy.8 = bf16[8,128,128]{1,0,2:T(8,128)(2,1)} copy(bf16[8,128,128]{2,1,0:T(8,128)(2,1)} %bitcast.6) | data formatting | bytes 524288 | tf_op jit(solution)/shard_map/reshape | solution.py:582
Async XLA Ops:
  0.0 2.0 %copy-start = (bf16[16,128,128]{2,1,0:T(8,128)(2,1)S(1)}, bf16[16,128,128]{2,1,0:T(8,128)(2,1)}, u32[]{:S(2)}) copy-start(bf16[16,128,128]{2,1,0:T(8,128)(2,1)} %f_ref.1) | copy-start | bytes 1572868

commit v5 on v4

--- a/solution.py
+++ b/solution.py
@@ -11,8 +11,8 @@
 
 
 def kernel(
-    virt, occ, pair, t_ref, ft_ref, f_ref, out_ref,
-    t_own, t_all, fca, fdb, ht, rp, ra1, ra2, rb1, rb2, rc1, rc2, own_in,
+    virt, occ, pair, t_ref, f_ref, out_ref,
+    t_own, f_own, ft_own, t_all, fca, fdb, ht, rp, ra1, ra2, rb1, rb2, rc1, rc2, own_in,
     send, recv,
 ):
     row, col = lax.axis_index("row"), lax.axis_index("col")
@@ -80,6 +80,9 @@
     def mask(p):
         return 0.5 + 0.5 * (two_rows(col) * (two(row) * pair_sign[p]))
 
+    fetched = pltpu.make_async_copy(f_ref, f_own, send.at[N_SEMS - 2])
+    fetched.start()
+
     barrier = pltpu.get_barrier_semaphore()
     for target in [*near["x"].values(), *near["y"].values(), *near["z"].values(), sibling, across_chip]:
         pl.semaphore_signal(barrier, inc=1, device_id=target, device_id_type=MESH)
@@ -263,10 +266,6 @@
     def b_done(s):
         for j in range(4):
             wait(("bx2", s, j), home)
-
-    given = put(ft_ref, fdb.at[xh, y, k], sibling, swapped)
-    kept = pltpu.make_async_copy(ft_ref, fdb.at[xh, y, k], send.at[N_SEMS - 1])
-    pl.when(home)(kept.start)
 
     def plane_own():
         pl.when(home)(given.wait_recv)
@@ -455,13 +454,24 @@
         pl.when(home)(lambda: write(lambda rows: rp[x // 2, y, x % 2, rows, :]))
 
     own_start(0)
+
+    fetched.wait()
+
+    @pl.loop(0, 16)
+    def _(q):
+        ft_own[q] = f_own[q].astype(jnp.float32).T.astype(jnp.bfloat16)
+
+    given = put(ft_own, fdb.at[xh, y, k], sibling, swapped)
+    kept = pltpu.make_async_copy(ft_own, fdb.at[xh, y, k], send.at[N_SEMS - 1])
+    pl.when(home)(kept.start)
+
     own_here(0)
     t_send(1)
     plane_own()
     own_start(1)
-    t_step(1)
     a_start(1)
     b_start(1)
+    t_step(1)
     own_here(1)
     a_x(1)
     f_send(1, 0)
@@ -511,14 +521,14 @@
     group_send(0)
     stage2(3, 5)
     group_send(1)
-    b_sum(0)
     f_step(4, 0)
     f_step(4, 1)
     stage2(5, 7)
     group_send(2)
-    b_sum(1)
+    b_sum(0)
     stage2(7, 8)
     group_send(3)
+    b_sum(1)
     b_sum(2)
     b_line(0)
     b_sum(3)
@@ -542,17 +552,19 @@
         when(condition, copy.wait_send)
 
 
-def ladder(virt, occ, pair, t, ft, f):
+def ladder(virt, occ, pair, t, f):
     bf16 = jnp.bfloat16
     hbm, vmem = pl.BlockSpec(memory_space=pl.ANY), pl.BlockSpec(memory_space=pltpu.VMEM)
     smem = pl.BlockSpec(memory_space=pltpu.SMEM)
     return pl.pallas_call(
         kernel,
         out_shape=jax.ShapeDtypeStruct((1024, 128), bf16),
-        in_specs=[smem, smem, smem, vmem, hbm, hbm],
+        in_specs=[smem, smem, smem, vmem, hbm],
         out_specs=vmem,
         scratch_shapes=[
             pltpu.VMEM((128, 1024), bf16),
+            pltpu.VMEM((16, 128, 128), bf16),
+            pltpu.VMEM((16, 128, 128), bf16),
             pltpu.VMEM((16, 128, 1024), bf16),
             pltpu.VMEM((16, 16, 128, 128), bf16),
             pltpu.VMEM((2, 4, 2, 16, 128, 128), bf16),
@@ -571,14 +583,13 @@
         compiler_params=pltpu.CompilerParams(
             collective_id=0, has_side_effects=True, vmem_limit_bytes=56 * 1024 * 1024
         ),
-    )(virt, occ, pair, t, ft, f)
+    )(virt, occ, pair, t, f)
 
 
 def on_device(amplitudes, factors, virt_irrep, occupied_symmetry_label, pair_index):
     rows, pairs, width = amplitudes.shape
     t = amplitudes.transpose(2, 1, 0)
-    ft = factors.transpose(0, 2, 1)
-    out = ladder(virt_irrep, occupied_symmetry_label, pair_index.T, t, ft, factors)
+    out = ladder(virt_irrep, occupied_symmetry_label, pair_index.T, t, factors)
     return out.reshape(pairs, width, rows).transpose(2, 0, 1)
 
 

time: 121 us -> 120 us (level)
    unnamed x4 -> x1, local copies, waits for them, and re-layouts: 2.96 us -> 1.9 us
where the time goes in v5:
time: 120 us
  Pallas kernels  116 us (97%)
  local copies, waits for them, and re-layouts  3.72 us (3%)
    pallas_call x1, Pallas kernels, ladder(): pl.pallas_call(kernel, out_shape=jax.ShapeDtypeStruct((1024, 128), bf16),...  116 us

profile of v5, /device:TPU:1, one launch (start us, length us, event | category | flops | bytes accessed | tf_op | source)
XLA Modules:
  0.0 120.2 jit_solution(15203609134382327146)
XLA Ops:
  0.0 1.9 %copy.6 = bf16[128,8,128]{0,1,2:T(8,128)(2,1)} copy(bf16[128,8,128]{2,1,0:T(8,128)(2,1)} %param.5) | data formatting | bytes 524288 | tf_op args[0]
  1.9 116.5 %shard_map.55 = bf16[1024,128]{1,0:T(8,128)(2,1)} custom-call(s32[32]{0:T(128)} %virt.1, s32[200]{0:T(256)} %occ.1, s32[2,8]{1,0:T(2,128)} %bitcast.6, bf16[128,8,128]{2,1,0:T(8,128)(2,1)} %bitcast.5, bf16[16,128,128]{2,1,0:T(8,128)(2,1)} %f_ref.1), custom_call_target="tpu_custom_call" | custom-call | tf_op jit(solution)/shard_map/pallas_call | solution.py:559
  118.4 1.8 %copy.7 = bf16[8,128,128]{1,0,2:T(8,128)(2,1)} copy(bf16[8,128,128]{2,1,0:T(8,128)(2,1)} %bitcast.4) | data formatting | bytes 524288 | tf_op jit(solution)/shard_map/reshape | solution.py:593
